TPU v7x, 32 devices: a whole 2x2x4 slice. The times are simulated.
32 devices in a mesh: noise: 4 (over y, x), nodes: 8 (over z, core).
Axes of the slice: x: 2, y: 2, z: 4, core: 2. Of those that a mesh axis runs over, the one named last changes fastest.
Arguments:
- inputs: bfloat16 [4, 8192, 512], P('noise', 'nodes'), may hold values from -6 to 6
- sigma: float32 [4], P('noise'), may hold values from 0.02 to 80
- neighbours: int32 [4, 8192, 16], P('noise', 'nodes'), may hold values from 0 to 8191, as said below
- cotangent: bfloat16 [4, 8192, 512], P('noise', 'nodes'), may hold values from -6 to 6
- inward_weight: float32 [512, 1536], P('nodes'), may hold values from -0.25 to 0.25
- inward_first: float32 [512, 1536], P('nodes'), may hold values from -512 to 512
- inward_second: float32 [512, 1536], P('nodes'), may hold values from 2730 to 10922
- outward_weight: float32 [512, 512], P('nodes'), may hold values from -0.5 to 0.5
- outward_first: float32 [512, 512], P('nodes'), may hold values from -512 to 512
- outward_second: float32 [512, 512], P('nodes'), may hold values from 2730 to 10922
- expand_weight: float32 [512, 2048], P('nodes'), may hold values from -0.25 to 0.25
- expand_first: float32 [512, 2048], P('nodes'), may hold values from -512 to 512
- expand_second: float32 [512, 2048], P('nodes'), may hold values from 2730 to 10922
- contract_weight: float32 [2048, 512], P('nodes'), may hold values from -0.25 to 0.25
- contract_first: float32 [2048, 512], P('nodes'), may hold values from -512 to 512
- contract_second: float32 [2048, 512], P('nodes'), may hold values from 2730 to 10922
- modulate_weight: float32 [512, 2048], P('nodes'), may hold values from -0.25 to 0.25
- modulate_first: float32 [512, 2048], P('nodes'), may hold values from -512 to 512
- modulate_second: float32 [512, 2048], P('nodes'), may hold values from 2730 to 10922
Outputs:
- outputs: bfloat16 [4, 8192, 512], P('noise', 'nodes')
- input_grad: float32 [4, 8192, 512], P('noise', 'nodes')
- inward_moment: float32 [512, 1536], P('nodes')
- inward_square: float32 [512, 1536], P('nodes')
- inward_fresh: float32 [512, 1536], P('nodes')
- outward_moment: float32 [512, 512], P('nodes')
- outward_square: float32 [512, 512], P('nodes')
- outward_fresh: float32 [512, 512], P('nodes')
- expand_moment: float32 [512, 2048], P('nodes')
- expand_square: float32 [512, 2048], P('nodes')
- expand_fresh: float32 [512, 2048], P('nodes')
- contract_moment: float32 [2048, 512], P('nodes')
- contract_square: float32 [2048, 512], P('nodes')
- contract_fresh: float32 [2048, 512], P('nodes')
- modulate_moment: float32 [512, 2048], P('nodes')
- modulate_square: float32 [512, 2048], P('nodes')
- modulate_fresh: float32 [512, 2048], P('nodes')
Inputs may be any that keep to these rules, and one draw needn't show every extreme that they name: `neighbours`: column 0 of node i is i itself, column 1 is (i + 64) mod 8192, column 2 is (i - 64) mod 8192; every neighbour of node i is (i + t) mod 8192 for some t with |t| <= 64.
All inputs are finite; a program needn't handle non-finite values.
Results may differ from a plain program's by a relative error of at most 0.017.
Values may be sent and summed in bfloat16 or wider, within the bound.
No kernel may reach another device: no remote copies, remote signals or barrier semaphores. Data moves between devices by JAX's collectives and lax.ppermute only.
A program may use at most 128 MiB of HBM per device.

v0:
```python
import math

import jax
import jax.numpy as jnp
from jax import lax
from jax.sharding import PartitionSpec as P

D = 512
HEADS = 4
NEIGH = 16
RIM = 64
STEP = 10
HEAD_DIM = 128


def padded(cells, sides, width):
    for axis, dim in sides:
        count = lax.axis_size(axis)
        head = lax.slice_in_dim(cells, 0, width, axis=dim)
        tail = lax.slice_in_dim(cells, cells.shape[dim] - width, cells.shape[dim], axis=dim)
        cells = jnp.concatenate(
            [
                lax.ppermute(tail, axis, [(i, (i + 1) % count) for i in range(count)]),
                cells,
                lax.ppermute(head, axis, [((i + 1) % count, i) for i in range(count)]),
            ],
            axis=dim,
        )
    return cells


def passed_along(value, axis, steps):
    count = lax.axis_size(axis)
    pairs = [(source, (source + steps) % count) for source in range(count)]
    return lax.ppermute(value, axis, pairs)


def fourier(sigma):
    half = D // 2
    counter = jnp.arange(half).astype(jnp.float32)
    freqs = jnp.exp(counter * (math.log(64.0) / (half - 1)))
    phase = jnp.log(sigma)[:, None] * freqs[None, :]
    return jnp.concatenate([jnp.sin(phase), jnp.cos(phase)], axis=-1)


def normalize_parts(values):
    center = values - jnp.mean(values, axis=-1, keepdims=True)
    inverse = lax.rsqrt(jnp.mean(center * center, axis=-1, keepdims=True) + 1e-06)
    return (center * inverse, inverse)


def norm_back(normed, inverse, grads):
    average = jnp.mean(grads, axis=-1, keepdims=True)
    along = jnp.mean(grads * normed, axis=-1, keepdims=True)
    return inverse * (grads - average - normed * along)


def rows_dot(left, right):
    return lax.dot_general(
        left, right, (((0,), (0,)), ((), ())), preferred_element_type=jnp.float32
    )


def back_dot(left, right):
    return lax.dot_general(
        left, right, (((1,), (1,)), ((), ())), preferred_element_type=jnp.float32
    )


def adamw(weight, first, second, grads):
    moment = 0.5 * first + 0.5 * grads
    square = 0.75 * second + 0.25 * grads * grads
    ratio = moment / (1.0 - 0.5**STEP) / (jnp.sqrt(square / (1.0 - 0.75**STEP)) + 1e-08)
    return (moment, square, weight - 0.02 * (ratio + 0.1 * weight))


def per_device(
    inputs,
    sigma,
    neighbours,
    cotangent,
    inward_weight,
    inward_first,
    inward_second,
    outward_weight,
    outward_first,
    outward_second,
    expand_weight,
    expand_first,
    expand_second,
    contract_weight,
    contract_first,
    contract_second,
    modulate_weight,
    modulate_first,
    modulate_second,
):
    w_in, w_out, w_exp, w_con, w_mod = (
        lax.all_gather(inward_weight.astype(jnp.bfloat16), "nodes", axis=0, tiled=True),
        lax.all_gather(outward_weight.astype(jnp.bfloat16), "nodes", axis=0, tiled=True),
        lax.all_gather(expand_weight.astype(jnp.bfloat16), "nodes", axis=0, tiled=True),
        lax.all_gather(contract_weight.astype(jnp.bfloat16), "nodes", axis=0, tiled=True),
        lax.all_gather(modulate_weight.astype(jnp.bfloat16), "nodes", axis=0, tiled=True),
    )
    states = inputs[0].astype(jnp.float32)
    rows, width = states.shape
    cond_low = fourier(sigma).astype(jnp.bfloat16)
    modulation = jnp.dot(cond_low, w_mod, preferred_element_type=jnp.float32)[0]
    scale_one = modulation[:width]
    shift_one = modulation[width : 2 * width]
    scale_two = modulation[2 * width : 3 * width]
    shift_two = modulation[3 * width :]
    normed_one, inverse_one = normalize_parts(states)
    first_in = (normed_one * (1.0 + scale_one) + shift_one).astype(jnp.bfloat16)
    joint = jnp.dot(first_in, w_in, preferred_element_type=jnp.float32).astype(jnp.bfloat16)
    queries = joint[:, :width]
    keyvals = joint[:, width:]
    widened = padded(keyvals, (("nodes", 0),), RIM)
    device = lax.axis_index("nodes")
    total = rows * lax.axis_size("nodes")
    places = (neighbours[0] - (device * rows - RIM)) % total
    block = math.gcd(rows, 512)
    count = rows // block
    window = block + 2 * RIM
    qblocks = queries.reshape(count, block, HEADS, HEAD_DIM)
    pblocks = places.reshape(count, block, NEIGH)

    def forward_block(pieces):
        qpart, ppart = pieces
        fetched = widened[ppart]
        kpart = fetched[..., :width].reshape(block, NEIGH, HEADS, HEAD_DIM)
        vpart = fetched[..., width:].reshape(block, NEIGH, HEADS, HEAD_DIM)
        scores = jnp.einsum(
            "bhd,bkhd->bkh", qpart, kpart, preferred_element_type=jnp.float32
        ) / math.sqrt(HEAD_DIM)
        top = jnp.max(scores, axis=1, keepdims=True)
        expo = jnp.exp(scores - top)
        probs = expo / jnp.sum(expo, axis=1, keepdims=True)
        result = jnp.einsum(
            "bkh,bkhd->bhd", probs.astype(jnp.bfloat16), vpart, preferred_element_type=jnp.float32
        )
        return (result.reshape(block, width), probs)

    attended, probs = lax.map(forward_block, (qblocks, pblocks))
    attended_low = attended.reshape(rows, width).astype(jnp.bfloat16)
    mixed = states + jnp.dot(attended_low, w_out, preferred_element_type=jnp.float32)
    normed_two, inverse_two = normalize_parts(mixed)
    second_in = (normed_two * (1.0 + scale_two) + shift_two).astype(jnp.bfloat16)
    up_act = jnp.dot(second_in, w_exp, preferred_element_type=jnp.float32)
    sigmoid_up = jax.nn.sigmoid(up_act)
    swished = (up_act * sigmoid_up).astype(jnp.bfloat16)
    final = mixed + jnp.dot(swished, w_con, preferred_element_type=jnp.float32)
    back_low = cotangent[0]
    grad_con = rows_dot(swished, back_low)
    d_swished = back_dot(back_low, w_con)
    d_up = (d_swished * sigmoid_up * (1.0 + up_act * (1.0 - sigmoid_up))).astype(jnp.bfloat16)
    grad_exp = rows_dot(second_in, d_up)
    d_second = back_dot(d_up, w_exp)
    d_scale_two = jnp.sum(d_second * normed_two, axis=0)
    d_shift_two = jnp.sum(d_second, axis=0)
    d_mixed = back_low.astype(jnp.float32) + norm_back(
        normed_two, inverse_two, d_second * (1.0 + scale_two)
    )
    d_mixed_low = d_mixed.astype(jnp.bfloat16)
    grad_out = rows_dot(attended_low, d_mixed_low)
    d_attended = back_dot(d_mixed_low, w_out).astype(jnp.bfloat16)
    dblocks = d_attended.reshape(count, block, HEADS, HEAD_DIM)
    slots = jnp.arange(window, dtype=jnp.int32)
    numbers = jnp.arange(count, dtype=jnp.int32)

    def backward_block(carry, pieces):
        qpart, ppart, prob, dpart, number = pieces
        base = number * block
        fetched = widened[ppart]
        vpart = fetched[..., width:].reshape(block, NEIGH, HEADS, HEAD_DIM)
        d_probs = jnp.einsum("bhd,bkhd->bkh", dpart, vpart, preferred_element_type=jnp.float32)
        d_scores = (
            prob * (d_probs - jnp.sum(prob * d_probs, axis=1, keepdims=True)) / math.sqrt(HEAD_DIM)
        )
        prob_low = prob.astype(jnp.bfloat16)
        onehot = ((ppart - base)[..., None] == slots).astype(jnp.bfloat16)
        score_band = jnp.einsum(
            "bkh,bkw->hbw", d_scores, onehot.astype(jnp.float32), precision=lax.Precision.HIGHEST
        )
        prob_band = jnp.einsum("bkh,bkw->hbw", prob_low, onehot, preferred_element_type=jnp.float32)
        local = lax.dynamic_slice_in_dim(widened, base, window, 0)
        local_keys = local[:, :width].reshape(window, HEADS, HEAD_DIM).astype(jnp.float32)
        d_query = jnp.einsum(
            "hbw,whd->bhd", score_band, local_keys, precision=lax.Precision.HIGHEST
        )
        d_key = jnp.einsum(
            "hbw,bhd->whd", score_band, qpart.astype(jnp.float32), precision=lax.Precision.HIGHEST
        )
        d_value = jnp.einsum(
            "hbw,bhd->whd", prob_band, dpart.astype(jnp.float32), precision=lax.Precision.HIGHEST
        )
        update = jnp.concatenate(
            [d_key.reshape(window, width), d_value.reshape(window, width)], axis=-1
        )
        current = lax.dynamic_slice_in_dim(carry, base, window, 0)
        carry = lax.dynamic_update_slice_in_dim(carry, current + update, base, 0)
        return (carry, d_query.reshape(block, width))

    start_grads = jnp.zeros((rows + 2 * RIM, 2 * width), jnp.float32)
    d_widened, d_queries = lax.scan(
        backward_block, start_grads, (qblocks, pblocks, probs, dblocks, numbers)
    )
    from_next = passed_along(d_widened[:RIM].astype(jnp.bfloat16), "nodes", -1).astype(jnp.float32)
    from_prev = passed_along(d_widened[rows + RIM :].astype(jnp.bfloat16), "nodes", 1).astype(
        jnp.float32
    )
    d_own = d_widened[RIM : RIM + rows]
    d_own = d_own.at[:RIM].add(from_prev)
    d_own = d_own.at[rows - RIM :].add(from_next)
    d_joint = jnp.concatenate([d_queries.reshape(rows, width), d_own], axis=-1).astype(jnp.bfloat16)
    grad_in = rows_dot(first_in, d_joint)
    d_first = back_dot(d_joint, w_in)
    d_scale_one = jnp.sum(d_first * normed_one, axis=0)
    d_shift_one = jnp.sum(d_first, axis=0)
    input_grad = d_mixed + norm_back(normed_one, inverse_one, d_first * (1.0 + scale_one))
    d_modulation = jnp.concatenate([d_scale_one, d_shift_one, d_scale_two, d_shift_two])[None, :]
    grad_mod = jnp.dot(
        cond_low.astype(jnp.float32).T, d_modulation, precision=lax.Precision.HIGHEST
    )
    summed = lax.psum((grad_in, grad_out, grad_exp, grad_con, grad_mod), "noise")
    shares = (
        lax.psum_scatter(summed[0], "nodes", scatter_dimension=0, tiled=True),
        lax.psum_scatter(summed[1], "nodes", scatter_dimension=0, tiled=True),
        lax.psum_scatter(summed[2], "nodes", scatter_dimension=0, tiled=True),
        lax.psum_scatter(summed[3], "nodes", scatter_dimension=0, tiled=True),
        lax.psum_scatter(summed[4], "nodes", scatter_dimension=0, tiled=True),
    )
    inward_new = adamw(inward_weight, inward_first, inward_second, shares[0])
    outward_new = adamw(outward_weight, outward_first, outward_second, shares[1])
    expand_new = adamw(expand_weight, expand_first, expand_second, shares[2])
    contract_new = adamw(contract_weight, contract_first, contract_second, shares[3])
    modulate_new = adamw(modulate_weight, modulate_first, modulate_second, shares[4])
    return (
        final.astype(jnp.bfloat16)[None],
        input_grad[None],
        inward_new[0],
        inward_new[1],
        inward_new[2],
        outward_new[0],
        outward_new[1],
        outward_new[2],
        expand_new[0],
        expand_new[1],
        expand_new[2],
        contract_new[0],
        contract_new[1],
        contract_new[2],
        modulate_new[0],
        modulate_new[1],
        modulate_new[2],
    )


def solution(mesh):
    placed = (
        P("noise", "nodes", None),
        P("noise"),
        P("noise", "nodes", None),
        P("noise", "nodes", None),
        P("nodes", None),
        P("nodes", None),
        P("nodes", None),
        P("nodes", None),
        P("nodes", None),
        P("nodes", None),
        P("nodes", None),
        P("nodes", None),
        P("nodes", None),
        P("nodes", None),
        P("nodes", None),
        P("nodes", None),
        P("nodes", None),
        P("nodes", None),
        P("nodes", None),
    )
    return jax.shard_map(
        per_device,
        mesh=mesh,
        in_specs=placed,
        out_specs=(
            P("noise", "nodes", None),
            P("noise", "nodes", None),
            P("nodes", None),
            P("nodes", None),
            P("nodes", None),
            P("nodes", None),
            P("nodes", None),
            P("nodes", None),
            P("nodes", None),
            P("nodes", None),
            P("nodes", None),
            P("nodes", None),
            P("nodes", None),
            P("nodes", None),
            P("nodes", None),
            P("nodes", None),
            P("nodes", None),
        ),
        check_vma=False,
    )
```

profile of v0, /device:TPU:0, one launch (start us, length us, event | category | flops | bytes accessed | tf_op | source)
XLA Modules:
  0.0 784.5 jit_solution(9739524806515107751)
XLA Ops:
  17.9 24.1 %all-gather.5.cloned.1.call-done = bf16[512,2048]{1,0:T(8,128)(2,1)} async-done(((bf16[64,2048]{1,0:T(8,128)(2,1)}), bf16[512,2048]{1,0:T(8,128)(2,1)}) %all-gather.5.cloned.1.call-update) | async-done | bytes 2097168 | tf_op jit(solution)/shard_map/all_gather | solution.py:103
  44.6 24.2 %all-gather.7.cloned.1.call-done = bf16[512,1536]{1,0:T(8,128)(2,1)} async-done(((bf16[64,1536]{1,0:T(8,128)(2,1)}), bf16[512,1536]{1,0:T(8,128)(2,1)}) %all-gather.7.cloned.1.call-update) | async-done | bytes 1572880 | tf_op jit(solution)/shard_map/all_gather | solution.py:99
  75.9 18.0 %all_gather.17 = bf16[512,512]{1,0:T(8,128)(2,1)} all-gather(bf16[64,512]{1,0:T(8,128)(2,1)S(1)} %convert_element_type.97), channel_id=1, replica_groups=mesh['noise'=4,'nodes'=8] {'nodes'}, dimensions={0}, use_global_device_ids=true | all-gather | bytes 589824 | tf_op jit(solution)/shard_map/all_gather | solution.py:100
  99.5 148.2 %while.27 = (s32[]{:T(128)}, bf16[2,512,512]{2,1,0:T(8,128)(2,1)}, f32[2,512,16,4]{1,3,2,0:T(4,128)}, s32[2,512,16]{2,1,0:T(8,128)S(1)}, bf16[1152,1024]{1,0:T(8...) while((s32[]{:T(128)}, bf16[2,512,512]{2,1,0:T(8,128)(2,1)}, f32[2,512,16,4]{1,3,2,0:T(4,128)}, ...), condition=%wide.region_5.6_spmd, body=%wide.region_2.5_spmd.sunk | while | flops 17199104 | bytes 92823680 | solution.py:144
  101.7 35.4 %gather_fusion = bf16[8192,1024]{1,0:T(8,128)(2,1)} fusion(bf16[1152,1024]{1,0:T(8,128)(2,1)S(1)} %get-tuple-element.413, s32[8192]{0:T(1024)S(1)} %broadcast_clamp_fusion.4), kind=kCustom, calls=%fused_computation.clone.1 | custom fusion | bytes 33587200 | tf_op jit(solution)/shard_map/while/body/eval_jaxpr/gather | solution.py:130
  137.1 12.8 %slice_bitcast_fusion.7 = (bf16[512,2,4,8,128]{4,3,2,1,0:T(8,128)(2,1)}, bf16[512,2,4,8,128]{4,3,2,1,0:T(8,128)(2,1)}) fusion(bf16[512,16,1024]{2,1,0:T(8,128)(2,1)} %bitcast.265), kind=kLoop, calls=%fused_computation.9.clone.1 | loop fusion | bytes 33554432 | tf_op jit(solution)/shard_map/while
  150.0 8.8 %fusion.140 = f32[512,4,1,16]{3,2,1,0:T(1,128)} fusion(bf16[512,2,4,8,128]{4,3,2,1,0:T(8,128)(2,1)} %get-tuple-element.382, bf16[512,4,128,1]{2,1,0,3:T(4,128)(2,1)S(1)} %copy-done.15), kind=kOutput, calls=%fused_computation.6.clone.1 | convolution fusion | flops 8388608 | bytes 9043968 | tf_op jit(solution)/shard_map/while/body/eval_jaxpr/bhd,bkhd->bkh/dot_general | solution.py:133
  163.9 7.0 fusion.142
  175.6 35.4 %gather_fusion = bf16[8192,1024]{1,0:T(8,128)(2,1)} fusion(bf16[1152,1024]{1,0:T(8,128)(2,1)S(1)} %get-tuple-element.413, s32[8192]{0:T(1024)S(1)} %broadcast_clamp_fusion.4), kind=kCustom, calls=%fused_computation.clone.1 | custom fusion | bytes 33587200 | tf_op jit(solution)/shard_map/while/body/eval_jaxpr/gather | solution.py:130
  211.0 12.8 %slice_bitcast_fusion.7 = (bf16[512,2,4,8,128]{4,3,2,1,0:T(8,128)(2,1)}, bf16[512,2,4,8,128]{4,3,2,1,0:T(8,128)(2,1)}) fusion(bf16[512,16,1024]{2,1,0:T(8,128)(2,1)} %bitcast.265), kind=kLoop, calls=%fused_computation.9.clone.1 | loop fusion | bytes 33554432 | tf_op jit(solution)/shard_map/while
  223.9 8.8 %fusion.140 = f32[512,4,1,16]{3,2,1,0:T(1,128)} fusion(bf16[512,2,4,8,128]{4,3,2,1,0:T(8,128)(2,1)} %get-tuple-element.382, bf16[512,4,128,1]{2,1,0,3:T(4,128)(2,1)S(1)} %copy-done.15), kind=kOutput, calls=%fused_computation.6.clone.1 | convolution fusion | flops 8388608 | bytes 9043968 | tf_op jit(solution)/shard_map/while/body/eval_jaxpr/bhd,bkhd->bkh/dot_general | solution.py:133
  237.8 7.0 fusion.142
  251.9 10.5 %multiply_convert_fusion.1 = (bf16[1024,2048]{1,0:T(8,128)(2,1)}, f32[1024,2048]{1,0:T(8,128)}) fusion(bf16[512,2048]{1,0:T(8,128)(2,1)} %all-gather.9.cloned.1.call-done, f32[1024,512]{0,1:T(8,128)} %copy-done.8, f32[512]{0:T(512)S(1)} %copy-done.61, f32[512]{0:T(512)S(1)} %copy-done.55, f32[1024]{0:T(1024)S(1)} %add_rsqrt_fusion, ...), kind=kOutput, calls=%fused_computation.63 | convolution fusion | flops 2160590848 | bytes 16789504 | tf_op jit(solution)/shard_map/dot_general | solution.py:149
  262.5 8.3 %multiply_convert_fusion = bf16[1024,2048]{1,0:T(8,128)(2,1)S(1)} fusion(f32[1024,2048]{1,0:T(8,128)} %get-tuple-element.288, bf16[2048,512]{1,0:T(8,128)(2,1)} %all-gather.11.cloned.1.call-done, bf16[1,1024,512]{2,1,0:T(8,128)(2,1)} %param.30), kind=kOutput, calls=%fused_computation.62 | convolution fusion | flops 2166358016 | bytes 15728640 | tf_op jit(solution)/shard_map/dot_general | solution.py:65
  295.9 179.6 %while.28 = (s32[]{:T(128)}, f32[1152,1024]{0,1:T(8,128)}, bf16[2,512,512]{2,1,0:T(8,128)(2,1)}, s32[2]{0:T(128)S(1)}, bf16[2,512,4,128]{3,2,1,0:T(4,128)(2,1)},...) while((s32[]{:T(128)}, f32[1152,1024]{0,1:T(8,128)}, ...), condition=%wide.region_12.13_spmd.clone, body=%wide.region_10.12_spmd.clone.sunk | while | flops 6353786880 | bytes 99991960 | solution.py:205
  310.5 4.7 fusion.153
  318.5 35.4 %gather_fusion.1 = bf16[8192,1024]{1,0:T(8,128)(2,1)} fusion(bf16[1152,1024]{1,0:T(8,128)(2,1)S(1)} %get-tuple-element.449, s32[8192]{0:T(1024)S(1)} %broadcast_clamp_fusion.5), kind=kCustom, calls=%fused_computation.1.clone.clone.1 | custom fusion | bytes 33587200 | tf_op jit(solution)/shard_map/while/body/eval_jaxpr/gather | solution.py:174
  353.9 9.1 %fusion.155 = f32[512,4,1,16]{3,2,1,0:T(1,128)} fusion(bf16[512,4,128,1]{2,3,1,0:T(2,128)(2,1)} %copy.152, bf16[512,16,1024]{2,1,0:T(8,128)(2,1)} %bitcast.266), kind=kOutput, calls=%fused_computation.29.clone.1 | convolution fusion | flops 8388608 | bytes 9568256 | tf_op jit(solution)/shard_map/while/body/eval_jaxpr/bhd,bkhd->bkh/dot_general | solution.py:176
  365.0 9.0 %fusion.157 = f32[4,512,640]{2,0,1:T(4,128)S(1)} fusion(s32[512,16]{1,0:T(8,128)S(1)} %copy-done.17, f32[1,512,16,4]{2,3,1,0:T(4,128)S(1)} %copy-done.1, f32[512,16,4]{1,2,0:T(4,128)S(1)} %bitcast.273, f32[512,4]{1,0:T(8,128)S(1)} %fusion.156), kind=kOutput, calls=%fused_computation.42.clone.1 | convolution fusion | flops 256999424 | bytes 5545984 | tf_op jit(solution)/shard_map/while/body/eval_jaxpr/bkh,bkw->hbw/dot_general | solution.py:182
  400.1 4.7 fusion.153
  408.1 35.4 %gather_fusion.1 = bf16[8192,1024]{1,0:T(8,128)(2,1)} fusion(bf16[1152,1024]{1,0:T(8,128)(2,1)S(1)} %get-tuple-element.449, s32[8192]{0:T(1024)S(1)} %broadcast_clamp_fusion.5), kind=kCustom, calls=%fused_computation.1.clone.clone.1 | custom fusion | bytes 33587200 | tf_op jit(solution)/shard_map/while/body/eval_jaxpr/gather | solution.py:174
  443.5 9.1 %fusion.155 = f32[512,4,1,16]{3,2,1,0:T(1,128)} fusion(bf16[512,4,128,1]{2,3,1,0:T(2,128)(2,1)} %copy.152, bf16[512,16,1024]{2,1,0:T(8,128)(2,1)} %bitcast.266), kind=kOutput, calls=%fused_computation.29.clone.1 | convolution fusion | flops 8388608 | bytes 9568256 | tf_op jit(solution)/shard_map/while/body/eval_jaxpr/bhd,bkhd->bkh/dot_general | solution.py:176
  454.6 9.0 %fusion.157 = f32[4,512,640]{2,0,1:T(4,128)S(1)} fusion(s32[512,16]{1,0:T(8,128)S(1)} %copy-done.17, f32[1,512,16,4]{2,3,1,0:T(4,128)S(1)} %copy-done.1, f32[512,16,4]{1,2,0:T(4,128)S(1)} %bitcast.273, f32[512,4]{1,0:T(8,128)S(1)} %fusion.156), kind=kOutput, calls=%fused_computation.42.clone.1 | convolution fusion | flops 256999424 | bytes 5545984 | tf_op jit(solution)/shard_map/while/body/eval_jaxpr/bkh,bkw->hbw/dot_general | solution.py:182
  504.2 6.6 fusion.57
  512.3 6.7 fusion.74
  519.0 5.6 fusion.86
  532.7 10.9 %reduce-scatter.6.cloned.1.call-done = f32[64,1536]{1,0:T(8,128)} async-done(((f32[512,1536]{1,0:T(8,128)}), f32[64,1536]{1,0:T(8,128)}) %reduce-scatter.6.cloned.1.call-update) | async-done | bytes 393232 | tf_op jit(solution)/shard_map/reduce_scatter | solution.py:227
  543.6 51.4 %reduce-scatter.12.cloned.1.call-done = f32[256,512]{1,0:T(8,128)} async-done(((f32[2048,512]{1,0:T(8,128)}), f32[256,512]{1,0:T(8,128)}) %reduce-scatter.12.cloned.1.call-update) | async-done | bytes 524304 | tf_op jit(solution)/shard_map/reduce_scatter | solution.py:230
  595.0 50.5 %reduce-scatter.10.cloned.1.call-done = f32[64,2048]{1,0:T(8,128)} async-done(((f32[512,2048]{1,0:T(8,128)}), f32[64,2048]{1,0:T(8,128)}) %reduce-scatter.10.cloned.1.call-update) | async-done | bytes 524304 | tf_op jit(solution)/shard_map/reduce_scatter | solution.py:229
  645.5 50.5 %reduce-scatter.14.cloned.1.call-done = f32[64,2048]{1,0:T(8,128)} async-done(((f32[512,2048]{1,0:T(8,128)}), f32[64,2048]{1,0:T(8,128)}) %reduce-scatter.14.cloned.1.call-update) | async-done | bytes 524304 | tf_op jit(solution)/shard_map/reduce_scatter | solution.py:231
  696.0 6.2 fusion.56
  711.5 56.5 %all-reduce.3.cloned.1.call-done = (f32[64,1536]{1,0:T(8,128)}, f32[64,512]{1,0:T(8,128)}, f32[64,2048]{1,0:T(8,128)}, f32[256,512]{1,0:T(8,128)}, f32[64,2048]{1,0:T(8,128)}) async-done(((f32[64,1536]{1,0:T(8,128)}, f32[64,512]{1,0:T(8,128)}, f32[64,2048]{1,0:T(8,128)}, f32[256,512]{1,0:T(8,128)}, f32[64,2048]{1,0:T(8,128)}), (f32[64,1536]{1,0:T(8,128)}, f32[64,512]{1,0:T(8,128)}, f32[64,2048]{1,0:T(8,128)}, ...) | async-done | bytes 2097168 | tf_op jit(solution)/shard_map/psum | solution.py:225
  (314 shorter events, 191.5 us)
Async XLA Ops:
  7.2 34.8 %all-gather.5.cloned.1.call-start = ((), (), s32[]{:S(2)}) async-start(), calls=%async_computation.5 | async-start | bytes 2359296 | tf_op jit(solution)/shard_map/all_gather | solution.py:103
  9.2 59.7 %all-gather.7.cloned.1.call-start = ((), (), s32[]{:S(2)}) async-start(), calls=%async_computation.6 | async-start | bytes 1769472 | tf_op jit(solution)/shard_map/all_gather | solution.py:99
  10.9 241.0 %all-gather.9.cloned.1.call-start = ((), (), s32[]{:S(2)}) async-start(), calls=%async_computation.7 | async-start | bytes 2359296 | tf_op jit(solution)/shard_map/all_gather | solution.py:101
  11.8 250.7 %all-gather.11.cloned.1.call-start = ((), (), s32[]{:S(2)}) async-start(), calls=%async_computation.8 | async-start | bytes 2359296 | tf_op jit(solution)/shard_map/all_gather | solution.py:102
  12.6 520.1 %reduce-scatter.8.cloned.1.call-start = ((), (), s32[]{:S(2)}) async-start(), calls=%async_computation.10 | async-start | bytes 1179648 | tf_op jit(solution)/shard_map/reduce_scatter | solution.py:228
  15.0 53.9 %copy-start.6 = (bf16[1,1024,512]{1,2,0:T(8,128)(2,1)}, bf16[1,1024,512]{1,2,0:T(8,128)(2,1)S(1)}, u32[]{:S(2)}) copy-start(bf16[1,1024,512]{1,2,0:T(8,128)(2,1)S(1)} %copy.57) | copy-start | bytes 3145732
  15.2 53.7 %copy-start.46 = (f32[1024]{0:T(1024)}, f32[1024]{0:T(1024)S(1)}, u32[]{:S(2)}) copy-start(f32[1024]{0:T(1024)S(1)} %broadcast_multiply_fusion.11) | copy-start | bytes 12292
  16.6 52.3 %copy-start.51 = (f32[1024]{0:T(1024)}, f32[1024]{0:T(1024)S(1)}, u32[]{:S(2)}) copy-start(f32[1024]{0:T(1024)S(1)} %add_rsqrt_fusion.1) | copy-start | bytes 12292
  44.6 27.7 %copy-start.57 = (f32[512]{0:T(512)}, f32[512]{0:T(512)S(1)}, u32[]{:S(2)}) copy-start(f32[512]{0:T(512)S(1)} %get-tuple-element.282) | copy-start | bytes 6148
  44.6 27.7 %copy-start.63 = (f32[512]{0:T(512)}, f32[512]{0:T(512)S(1)}, u32[]{:S(2)}) copy-start(f32[512]{0:T(512)S(1)} %get-tuple-element.281) | copy-start | bytes 6148
  72.3 24.3 %collective-permute-start = (bf16[64,1024]{1,0:T(8,128)(2,1)S(1)}, bf16[64,1024]{1,0:T(8,128)(2,1)S(1)}, u32[]{:S(2)}, u32[]{:S(2)}) collective-permute-start(bf16[64,1024]{1,0:T(8,128)(2,1)S(1)} %get-tuple-element.270), channel_id=1, source_target_pairs={{0,1},{1,2},{2,3},{3,4},{4,5},{5,6},{6,7},{7,0},{8,9},{9,10},{10,1... | collective-permute-start | bytes 393224 | tf_op jit(solution)/shard_map/ppermute | solution.py:23
  72.6 24.1 %collective-permute-start.1 = (bf16[64,1024]{1,0:T(8,128)(2,1)S(1)}, bf16[64,1024]{1,0:T(8,128)(2,1)S(1)}, u32[]{:S(2)}, u32[]{:S(2)}) collective-permute-start(bf16[64,1024]{1,0:T(8,128)(2,1)S(1)} %get-tuple-element.271), channel_id=1, source_target_pairs={{1,0},{2,1},{3,2},{4,3},{5,4},{6,5},{7,6},{0,7},{9,8},{10,9},{11,1... | collective-permute-start | bytes 393224 | tf_op jit(solution)/shard_map/ppermute | solution.py:25
  137.1 12.8 %copy-start.15 = (bf16[512,4,128,1]{2,1,0,3:T(4,128)(2,1)S(1)}, bf16[512,4,128,1]{2,1,0,3:T(4,128)(2,1)}, u32[]{:S(2)}) copy-start(bf16[512,4,128,1]{2,1,0,3:T(4,128)(2,1)} %dynamic-slice_bitcast_fusion.2) | copy-start | bytes 1572868 | tf_op jit(solution)/shard_map/while
  250.3 31.3 %copy-start.48 = (f32[1024]{0:T(1024)}, f32[1024]{0:T(1024)S(1)}, u32[]{:S(2)}) copy-start(f32[1024]{0:T(1024)S(1)} %broadcast_multiply_fusion.10) | copy-start | bytes 12292
  251.9 29.8 %copy-start.53 = (f32[1024]{0:T(1024)}, f32[1024]{0:T(1024)S(1)}, u32[]{:S(2)}) copy-start(f32[1024]{0:T(1024)S(1)} %add_rsqrt_fusion) | copy-start | bytes 12292
  290.2 253.4 %reduce-scatter.6.cloned.1.call-start = ((), (), s32[]{:S(2)}) async-start(), calls=%async_computation.9 | async-start | bytes 3538944 | tf_op jit(solution)/shard_map/reduce_scatter | solution.py:227
  478.4 7.6 collective-permute-start.2
  482.9 15.1 %copy-start.30 = (bf16[1024,512]{0,1:T(8,128)(2,1)}, bf16[1024,512]{0,1:T(8,128)(2,1)S(1)}, u32[]{:S(2)}) copy-start(bf16[1024,512]{0,1:T(8,128)(2,1)S(1)} %copy.67) | copy-start | bytes 3145732
  482.9 7.9 %collective-permute-start.3 = (bf16[64,1024]{0,1:T(8,128)(2,1)S(1)}, bf16[64,1024]{0,1:T(8,128)(2,1)S(1)}, u32[]{:S(2)}, u32[]{:S(2)}) collective-permute-start(bf16[64,1024]{0,1:T(8,128)(2,1)S(1)} %get-tuple-element.272), channel_id=1, source_target_pairs={{0,7},{1,0},{2,1},{3,2},{4,3},{5,4},{6,5},{7,6},{8,15},{9,8},{10,9... | collective-permute-start | bytes 393224 | tf_op jit(solution)/shard_map/ppermute | solution.py:35
  503.0 92.0 %reduce-scatter.12.cloned.1.call-start = ((), (), s32[]{:S(2)}) async-start(), calls=%async_computation.12 | async-start | bytes 4718592 | tf_op jit(solution)/shard_map/reduce_scatter | solution.py:230
  510.8 134.7 %reduce-scatter.10.cloned.1.call-start = ((), (), s32[]{:S(2)}) async-start(), calls=%async_computation.11 | async-start | bytes 4718592 | tf_op jit(solution)/shard_map/reduce_scatter | solution.py:229
  519.0 176.9 %reduce-scatter.14.cloned.1.call-start = ((), (), s32[]{:S(2)}) async-start(), calls=%async_computation.13 | async-start | bytes 4718592 | tf_op jit(solution)/shard_map/reduce_scatter | solution.py:231
  532.6 235.4 %all-reduce.3.cloned.1.call-start = ((), (), s32[]{:S(2)}) async-start(), calls=%async_computation.14 | async-start | bytes 4194304 | tf_op jit(solution)/shard_map/psum | solution.py:225
  708.4 59.6 %copy-start.41 = (f32[64,512]{1,0:T(8,128)S(1)}, f32[64,512]{1,0:T(8,128)}, u32[]{:S(2)}) copy-start(f32[64,512]{1,0:T(8,128)} %param.34) | copy-start | bytes 393220
  708.4 59.6 %copy-start.44 = (f32[64,512]{1,0:T(8,128)S(1)}, f32[64,512]{1,0:T(8,128)}, u32[]{:S(2)}) copy-start(f32[64,512]{1,0:T(8,128)} %param.35) | copy-start | bytes 393220
  708.4 59.6 %copy-start.45 = (f32[64,512]{1,0:T(8,128)S(1)}, f32[64,512]{1,0:T(8,128)}, u32[]{:S(2)}) copy-start(f32[64,512]{1,0:T(8,128)} %param.36) | copy-start | bytes 393220
  708.4 61.4 %copy-start.26 = (f32[64,1536]{1,0:T(8,128)S(1)}, f32[64,1536]{1,0:T(8,128)}, u32[]{:S(2)}) copy-start(f32[64,1536]{1,0:T(8,128)} %param.31) | copy-start | bytes 1179652
  708.4 61.4 %copy-start.42 = (f32[64,1536]{1,0:T(8,128)S(1)}, f32[64,1536]{1,0:T(8,128)}, u32[]{:S(2)}) copy-start(f32[64,1536]{1,0:T(8,128)} %param.32) | copy-start | bytes 1179652
  708.4 61.4 %copy-start.43 = (f32[64,1536]{1,0:T(8,128)S(1)}, f32[64,1536]{1,0:T(8,128)}, u32[]{:S(2)}) copy-start(f32[64,1536]{1,0:T(8,128)} %param.33) | copy-start | bytes 1179652
  711.5 60.7 %copy-start.22 = (f32[64,2048]{1,0:T(8,128)S(1)}, f32[64,2048]{1,0:T(8,128)}, u32[]{:S(2)}) copy-start(f32[64,2048]{1,0:T(8,128)} %param.37) | copy-start | bytes 1572868
  711.5 60.7 %copy-start.31 = (f32[64,2048]{1,0:T(8,128)S(1)}, f32[64,2048]{1,0:T(8,128)}, u32[]{:S(2)}) copy-start(f32[64,2048]{1,0:T(8,128)} %param.38) | copy-start | bytes 1572868
  711.5 60.7 %copy-start.32 = (f32[64,2048]{1,0:T(8,128)S(1)}, f32[64,2048]{1,0:T(8,128)}, u32[]{:S(2)}) copy-start(f32[64,2048]{1,0:T(8,128)} %param.39) | copy-start | bytes 1572868
  (58 other events, 201.7 us)
Sparse Core Ops, SparseCore 0:
  10.2 31.7 all-gather.4
  44.3 24.5 all-gather.6
  71.0 31.5 all-gather.8
  104.7 29.1 all-gather.10
  290.3 32.0 reduce-scatter.7
  503.1 40.4 reduce-scatter.5
  545.9 49.0 reduce-scatter.11
  597.3 48.1 reduce-scatter.9
  647.8 48.1 reduce-scatter.13
  699.3 68.6 all-reduce.2
where the time goes:
time: 790 us; the launch traced here: 784 us
  waiting for transfers between devices  269 us (34%)
  local copies, waits for them, and re-layouts  255 us (32%)
  matrix products  161 us (20%)
  other arithmetic  56 us (7%)
  blocking collectives  18 us (2%)
  between operations  16 us (2%)
    gather x2, local copies, waits for them, and re-layouts, forward_block(): fetched = widened[ppart]  70.8 us
    gather x2, local copies, waits for them, and re-layouts, backward_block(): fetched = widened[ppart]  70.8 us
    psum x1, waiting for transfers between devices, per_device(): lax.psum((grad_in, grad_out, grad_exp, grad_con, grad_mod), 'noise')  56.5 us
    reduce_scatter x1, waiting for transfers between devices, per_device(): lax.psum_scatter(summed[3], 'nodes', scatter_dimension=0, tiled=True)  51.4 us
    reduce_scatter x1, waiting for transfers between devices, per_device(): lax.psum_scatter(summed[2], 'nodes', scatter_dimension=0, tiled=True)  50.5 us
    reduce_scatter x1, waiting for transfers between devices, per_device(): lax.psum_scatter(summed[4], 'nodes', scatter_dimension=0, tiled=True)  50.5 us
    while x34, local copies, waits for them, and re-layouts  25.8 us
    all_gather x1, waiting for transfers between devices, per_device(): lax.all_gather(inward_weight.astype(jnp.bfloat16), 'nodes', axis=0, tiled...  24.2 us
  transfers between devices with their start and end apart: 14, of which 8 were waited for; matrix products, arithmetic and copies ran while one was open for 54% of the time, Pallas kernels for 0%

commit v1 on v0

v1 whole, which is shorter than its diff:
```python
import functools
import math

import jax
import jax.numpy as jnp
from jax import lax
from jax.experimental import pallas as pl
from jax.experimental.pallas import tpu as pltpu
from jax.sharding import PartitionSpec as P

D = 512
HEADS = 4
NEIGH = 16
RIM = 64
STEP = 10
HEAD_DIM = 128
BLOCK = 128
WINDOW = BLOCK + 2 * RIM
AXES = ("noise", "nodes")
BF16 = jnp.bfloat16
F32 = jnp.float32
NONE = -1e30


def dot(left, right, left_dim, right_dim):
    return lax.dot_general(
        left, right, (((left_dim,), (right_dim,)), ((), ())), preferred_element_type=F32
    )


def fourier(sigma):
    half = D // 2
    counter = jnp.arange(half).astype(F32)
    freqs = jnp.exp(counter * (math.log(64.0) / (half - 1)))
    phase = jnp.log(sigma)[:, None] * freqs[None, :]
    return jnp.concatenate([jnp.sin(phase), jnp.cos(phase)], axis=-1)


def normalize_parts(values):
    center = values - jnp.mean(values, axis=-1, keepdims=True)
    inverse = lax.rsqrt(jnp.mean(center * center, axis=-1, keepdims=True) + 1e-06)
    return (center * inverse, inverse)


def norm_back(normed, inverse, grads):
    average = jnp.mean(grads, axis=-1, keepdims=True)
    along = jnp.mean(grads * normed, axis=-1, keepdims=True)
    return inverse * (grads - average - normed * along)


def adamw(weight, first, second, grads):
    moment = 0.5 * first + 0.5 * grads
    square = 0.75 * second + 0.25 * grads * grads
    ratio = moment / (1.0 - 0.5**STEP) / (jnp.sqrt(square / (1.0 - 0.75**STEP)) + 1e-08)
    return (moment, square, weight - 0.02 * (ratio + 0.1 * weight))


def params(mib, grid=1):
    return pltpu.CompilerParams(
        vmem_limit_bytes=mib * 2**20, dimension_semantics=("arbitrary",) * grid
    )


def cost(flops, moved):
    return pl.CostEstimate(flops=flops, bytes_accessed=moved, transcendentals=0)


def count_kernel(places_ref, bias_ref):
    places = places_ref[...]
    lanes = lax.broadcasted_iota(jnp.int32, (BLOCK, WINDOW), 1)
    count = jnp.zeros((BLOCK, WINDOW), F32)
    for k in range(NEIGH):
        count = count + (places[:, k : k + 1] == lanes).astype(F32)
    bias_ref[...] = jnp.where(count > 0.0, jnp.log(count), NONE)


def count_call(places):
    rows = places.shape[0]
    return pl.pallas_call(
        count_kernel,
        grid=(rows // BLOCK,),
        in_specs=[pl.BlockSpec((BLOCK, NEIGH), lambda i: (i, 0))],
        out_specs=pl.BlockSpec((BLOCK, WINDOW), lambda i: (i, 0)),
        out_shape=jax.ShapeDtypeStruct((rows, WINDOW), F32),
        compiler_params=params(32),
        cost_estimate=cost(rows * WINDOW * 48, rows * WINDOW * 4),
        name="neighbour_counts",
    )(places)


def attend_kernel(q_ref, low_ref, high_ref, bias_ref, out_ref, probs_ref):
    bias = bias_ref[...]
    scale = 1.0 / math.sqrt(HEAD_DIM)
    for h in range(HEADS):
        cols = slice(h * HEAD_DIM, (h + 1) * HEAD_DIM)
        vals = slice(D + h * HEAD_DIM, D + (h + 1) * HEAD_DIM)
        keys = jnp.concatenate([low_ref[:, cols], high_ref[:, cols]], axis=0)
        values = jnp.concatenate([low_ref[:, vals], high_ref[:, vals]], axis=0)
        scores = dot(q_ref[:, cols], keys, 1, 1) * scale + bias
        top = jnp.max(scores, axis=1, keepdims=True)
        expo = jnp.exp(scores - top)
        probs = (expo * (1.0 / jnp.sum(expo, axis=1, keepdims=True))).astype(BF16)
        probs_ref[:, h * WINDOW : (h + 1) * WINDOW] = probs
        out_ref[:, cols] = dot(probs, values, 1, 0).astype(BF16)


def attend_call(queries, keyvals, bias):
    rows = queries.shape[0]
    return pl.pallas_call(
        attend_kernel,
        grid=(rows // BLOCK,),
        in_specs=[
            pl.BlockSpec((BLOCK, D), lambda i: (i, 0)),
            pl.BlockSpec((BLOCK, 2 * D), lambda i: (i, 0)),
            pl.BlockSpec((BLOCK, 2 * D), lambda i: (i + 1, 0)),
            pl.BlockSpec((BLOCK, WINDOW), lambda i: (i, 0)),
        ],
        out_specs=[
            pl.BlockSpec((BLOCK, D), lambda i: (i, 0)),
            pl.BlockSpec((BLOCK, HEADS * WINDOW), lambda i: (i, 0)),
        ],
        out_shape=[
            jax.ShapeDtypeStruct((rows, D), BF16),
            jax.ShapeDtypeStruct((rows, HEADS * WINDOW), BF16),
        ],
        compiler_params=params(32),
        cost_estimate=cost(4 * rows * WINDOW * D, 6 * 2**20),
        name="attention_forward",
    )(queries, keyvals, keyvals, bias)


def attend_back_kernel(
    q_ref, low_ref, high_ref, probs_ref, grad_ref, dq_ref, dkv_ref, carry_ref
):
    step = pl.program_id(0)
    last = pl.num_programs(0) - 1
    scale = 1.0 / math.sqrt(HEAD_DIM)

    @pl.when(step == 0)
    def _():
        carry_ref[...] = jnp.zeros_like(carry_ref)

    @pl.when(step == last)
    def _():
        dkv_ref[...] = carry_ref[...].astype(BF16)

    @pl.when(step < last)
    def _():
        for h in range(HEADS):
            cols = slice(h * HEAD_DIM, (h + 1) * HEAD_DIM)
            vals = slice(D + h * HEAD_DIM, D + (h + 1) * HEAD_DIM)
            keys = jnp.concatenate([low_ref[:, cols], high_ref[:, cols]], axis=0)
            values = jnp.concatenate([low_ref[:, vals], high_ref[:, vals]], axis=0)
            grads = grad_ref[:, cols]
            probs = probs_ref[:, h * WINDOW : (h + 1) * WINDOW]
            wide = probs.astype(F32)
            d_probs = dot(grads, values, 1, 1)
            weighted = wide * d_probs
            total = jnp.sum(weighted, axis=1, keepdims=True)
            d_scores = ((weighted - wide * total) * scale).astype(BF16)
            dq_ref[:, cols] = dot(d_scores, keys, 1, 0).astype(BF16)
            d_keys = dot(d_scores, q_ref[:, cols], 0, 0)
            d_values = dot(probs, grads, 0, 0)
            dkv_ref[:, cols] = (carry_ref[:, cols] + d_keys[:BLOCK]).astype(BF16)
            dkv_ref[:, vals] = (carry_ref[:, vals] + d_values[:BLOCK]).astype(BF16)
            carry_ref[:, cols] = d_keys[BLOCK:]
            carry_ref[:, vals] = d_values[BLOCK:]


def attend_back_call(queries, keyvals, probs, grads):
    rows = queries.shape[0]
    count = rows // BLOCK
    here = lambda i: (jnp.minimum(i, count - 1), 0)
    return pl.pallas_call(
        attend_back_kernel,
        grid=(count + 1,),
        in_specs=[
            pl.BlockSpec((BLOCK, D), here),
            pl.BlockSpec((BLOCK, 2 * D), here),
            pl.BlockSpec((BLOCK, 2 * D), lambda i: (jnp.minimum(i + 1, count), 0)),
            pl.BlockSpec((BLOCK, HEADS * WINDOW), here),
            pl.BlockSpec((BLOCK, D), here),
        ],
        out_specs=[
            pl.BlockSpec((BLOCK, D), here),
            pl.BlockSpec((BLOCK, 2 * D), lambda i: (i, 0)),
        ],
        out_shape=[
            jax.ShapeDtypeStruct((rows, D), BF16),
            jax.ShapeDtypeStruct((rows + 2 * RIM, 2 * D), BF16),
        ],
        scratch_shapes=[pltpu.VMEM((BLOCK, 2 * D), F32)],
        compiler_params=params(32),
        cost_estimate=cost(8 * rows * WINDOW * D, 10 * 2**20),
        name="attention_backward",
    )(queries, keyvals, keyvals, probs, grads)


ROWS_MLP = 256
CHUNK = 512


def mlp_kernel(
    attended_ref, states_ref, cot_ref, mod_ref, w_out_ref, w_exp_ref, w_con_ref,
    final_ref, second_ref, swished_ref, d_up_ref, d_mixed_ref, d_att_ref, sums_ref,
):
    scale_two = mod_ref[2:3, :]
    shift_two = mod_ref[3:4, :]
    cot = cot_ref[...]
    mixed = states_ref[...].astype(F32) + dot(attended_ref[...], w_out_ref[...], 1, 0)
    normed, inverse = normalize_parts(mixed)
    second_in = (normed * (1.0 + scale_two) + shift_two).astype(BF16)
    second_ref[...] = second_in
    hidden = w_exp_ref.shape[1]
    final = mixed
    d_second = jnp.zeros_like(mixed)
    for start in range(0, hidden, CHUNK):
        part = slice(start, start + CHUNK)
        up = dot(second_in, w_exp_ref[:, part], 1, 0)
        gate = 0.5 + 0.5 * jnp.tanh(0.5 * up)
        product = up * gate
        swished = product.astype(BF16)
        swished_ref[:, part] = swished
        final = final + dot(swished, w_con_ref[part, :], 1, 0)
        d_swished = dot(cot, w_con_ref[part, :], 1, 1)
        d_up = (d_swished * (gate + product * (1.0 - gate))).astype(BF16)
        d_up_ref[:, part] = d_up
        d_second = d_second + dot(d_up, w_exp_ref[:, part], 1, 1)
    final_ref[...] = final.astype(BF16)

    @pl.when(pl.program_id(0) == 0)
    def _():
        sums_ref[...] = jnp.zeros_like(sums_ref)

    sums_ref[0:1, :] += jnp.sum(d_second * normed, axis=0, keepdims=True)
    sums_ref[1:2, :] += jnp.sum(d_second, axis=0, keepdims=True)
    d_mixed = cot.astype(F32) + norm_back(normed, inverse, d_second * (1.0 + scale_two))
    d_mixed_ref[...] = d_mixed
    d_att_ref[...] = dot(d_mixed.astype(BF16), w_out_ref[...], 1, 1).astype(BF16)


def mlp_call(attended, states, cot, mod, w_out, w_exp, w_con):
    rows = states.shape[0]
    hidden = w_exp.shape[1]
    some = lambda width: pl.BlockSpec((ROWS_MLP, width), lambda i: (i, 0))
    whole = lambda array: pl.BlockSpec(array.shape, lambda i: (0, 0))
    return pl.pallas_call(
        mlp_kernel,
        grid=(rows // ROWS_MLP,),
        in_specs=[some(D), some(D), some(D), whole(mod), whole(w_out), whole(w_exp), whole(w_con)],
        out_specs=[
            some(D), some(D), some(hidden), some(hidden), some(D), some(D),
            pl.BlockSpec((8, D), lambda i: (0, 0)),
        ],
        out_shape=[
            jax.ShapeDtypeStruct((rows, D), BF16),
            jax.ShapeDtypeStruct((rows, D), BF16),
            jax.ShapeDtypeStruct((rows, hidden), BF16),
            jax.ShapeDtypeStruct((rows, hidden), BF16),
            jax.ShapeDtypeStruct((rows, D), F32),
            jax.ShapeDtypeStruct((rows, D), BF16),
            jax.ShapeDtypeStruct((8, D), F32),
        ],
        compiler_params=params(48),
        cost_estimate=cost(rows * D * (8 * hidden + 4 * D), 22 * 2**20),
        name="mlp",
    )(attended, states, cot, mod, w_out, w_exp, w_con)


def first_kernel(dq_ref, dkv_ref, states_ref, d_mixed_ref, mod_ref, w_in_ref, grad_ref, sums_ref):
    scale_one = mod_ref[0:1, :]
    normed, inverse = normalize_parts(states_ref[...].astype(F32))
    d_first = dot(dq_ref[...], w_in_ref[:, :D], 1, 1) + dot(dkv_ref[...], w_in_ref[:, D:], 1, 1)

    @pl.when(pl.program_id(0) == 0)
    def _():
        sums_ref[...] = jnp.zeros_like(sums_ref)

    sums_ref[0:1, :] += jnp.sum(d_first * normed, axis=0, keepdims=True)
    sums_ref[1:2, :] += jnp.sum(d_first, axis=0, keepdims=True)
    grad_ref[...] = d_mixed_ref[...] + norm_back(normed, inverse, d_first * (1.0 + scale_one))


def first_call(dq, dkv, states, d_mixed, mod, w_in):
    rows = states.shape[0]
    some = lambda width: pl.BlockSpec((ROWS_MLP, width), lambda i: (i, 0))
    whole = lambda array: pl.BlockSpec(array.shape, lambda i: (0, 0))
    return pl.pallas_call(
        first_kernel,
        grid=(rows // ROWS_MLP,),
        in_specs=[some(D), some(2 * D), some(D), some(D), whole(mod), whole(w_in)],
        out_specs=[some(D), pl.BlockSpec((8, D), lambda i: (0, 0))],
        out_shape=[jax.ShapeDtypeStruct((rows, D), F32), jax.ShapeDtypeStruct((8, D), F32)],
        compiler_params=params(32),
        cost_estimate=cost(2 * rows * D * 3 * D, 10 * 2**20),
        name="input_gradient",
    )(dq, dkv, states, d_mixed, mod, w_in)


class Layout:
    def __init__(self):
        self.noise = lax.axis_size("noise")
        self.nodes = lax.axis_size("nodes")
        self.chips = self.nodes // 2

    def permute(self, value, move):
        pairs = []
        for n in range(self.noise):
            for z in range(self.chips):
                for c in range(2):
                    n2, z2, c2 = move(n, z % self.chips, c)
                    source = (n * self.chips + z) * 2 + c
                    target = (n2 * self.chips + z2 % self.chips) * 2 + c2
                    pairs.append((source, target))
        return lax.ppermute(value, AXES, pairs)

    def along(self, value, steps):
        count = self.nodes
        return lax.ppermute(value, "nodes", [(i, (i + steps) % count) for i in range(count)])

    def sum_nodes(self, value):
        value = value + self.permute(value, lambda n, z, c: (n, z, 1 - c))
        bit = 1
        while bit < self.chips:
            value = value + self.permute(value, lambda n, z, c: (n, z ^ bit, c))
            bit *= 2
        return value

    def gather_noise(self, value):
        n = lax.axis_index("noise")
        held = value[None]
        bit = 1
        while bit < self.noise:
            held = jnp.concatenate(
                [held, self.permute(held, lambda m, z, c: (m ^ bit, z, c))], axis=0
            )
            bit *= 2
        order = jnp.arange(self.noise) ^ n
        return held[order]

    def reduce_rows(self, grads):
        rows, cols = grads.shape
        own = rows // self.nodes
        part = cols // self.noise
        me = lax.axis_index("nodes")
        c = me % 2
        z = me // 2
        n = lax.axis_index("noise")
        blocks = grads.astype(BF16).reshape(self.chips, 2, own, cols)
        mine = lax.dynamic_index_in_dim(blocks, c, 1, keepdims=False)
        theirs = lax.dynamic_index_in_dim(blocks, 1 - c, 1, keepdims=False)
        got = self.permute(theirs, lambda n, z, c: (n, z, 1 - c))
        held = (mine.astype(F32) + got.astype(F32)).astype(BF16)
        held = held.reshape(self.chips, own, self.noise, part).transpose(2, 0, 1, 3)
        low, high = n % 2, n // 2
        slots = []
        for i in range(2):
            for j in range(2):
                at_zero = ((high ^ j) * 2) + (low ^ i)
                at_one = ((high ^ i) * 2) + (low ^ j)
                slots.append(held[jnp.where(c == 0, at_zero, at_one)])
        first_move = lambda n, z, c: (n ^ (1 if c == 0 else 2), z, c)
        second_move = lambda n, z, c: (n ^ (2 if c == 0 else 1), z, c)
        kept = jnp.stack(slots[:2]).astype(F32)
        kept = kept + self.permute(jnp.stack(slots[2:]), first_move).astype(F32)
        total = kept[0] + self.permute(kept[1].astype(BF16), second_move).astype(F32)
        total = jnp.roll(total, -z, axis=0)
        result = total[0]
        for s in range(1, self.chips):
            piece = total[s].astype(BF16)
            result = result + self.permute(piece, lambda n, z, c: (n, z + s, c)).astype(F32)
        result = result.astype(BF16)
        pair = jnp.stack([result, self.permute(result, second_move)])
        other = self.permute(pair, first_move)
        quarters = [pair[0], pair[1], other[0], other[1]]
        stacked = jnp.stack(quarters)
        order = []
        for q in range(4):
            x, y = q % 2, q // 2
            i = jnp.where(c == 0, x ^ low, y ^ high)
            j = jnp.where(c == 0, y ^ high, x ^ low)
            order.append(stacked[i * 2 + j])
        return jnp.concatenate(order, axis=-1).astype(F32)


def per_device(
    inputs, sigma, neighbours, cotangent,
    inward_weight, inward_first, inward_second,
    outward_weight, outward_first, outward_second,
    expand_weight, expand_first, expand_second,
    contract_weight, contract_first, contract_second,
    modulate_weight, modulate_first, modulate_second,
):
    net = Layout()
    states_low = inputs[0]
    cot = cotangent[0]
    rows = states_low.shape[0]
    device = lax.axis_index("nodes")
    own = modulate_weight.shape[0]

    w_in = lax.all_gather(inward_weight.astype(BF16), "nodes", axis=0, tiled=True)
    w_out = lax.all_gather(outward_weight.astype(BF16), "nodes", axis=0, tiled=True)
    w_exp = lax.all_gather(expand_weight.astype(BF16), "nodes", axis=0, tiled=True)
    w_con = lax.all_gather(contract_weight.astype(BF16), "nodes", axis=0, tiled=True)

    before = net.along(states_low[rows - RIM :], 1)
    after = net.along(states_low[:RIM], -1)

    cond_low = fourier(sigma).astype(BF16)
    cond_part = lax.dynamic_slice_in_dim(cond_low, device * own, own, 1)
    partial = jnp.dot(cond_part, modulate_weight.astype(BF16), preferred_element_type=F32)
    mod = net.sum_nodes(partial.reshape(4, D))

    total = rows * net.nodes
    place = (neighbours[0] - (device * rows - RIM)) % total
    place = place - (jnp.arange(rows, dtype=jnp.int32) // BLOCK * BLOCK)[:, None]
    bias = count_call(place)

    wide = jnp.concatenate([before, states_low, after], axis=0).astype(F32)
    normed, _ = normalize_parts(wide)
    first_in = (normed * (1.0 + mod[0:1]) + mod[1:2]).astype(BF16)
    queries = dot(first_in[RIM : RIM + rows], w_in[:, :D], 1, 0).astype(BF16)
    keyvals = dot(first_in, w_in[:, D:], 1, 0).astype(BF16)

    attended, probs = attend_call(queries, keyvals, bias)
    final, second_in, swished, d_up, d_mixed, d_attended, sums_two = mlp_call(
        attended, states_low, cot, mod, w_out, w_exp, w_con
    )
    grad_con = dot(swished, cot, 0, 0)
    grad_exp = dot(second_in, d_up, 0, 0)
    grad_out = dot(attended, d_mixed.astype(BF16), 0, 0)
    dq, dkv_wide = attend_back_call(queries, keyvals, probs, d_attended)
    grad_in = jnp.concatenate(
        [dot(first_in[RIM : RIM + rows], dq, 0, 0), dot(first_in, dkv_wide, 0, 0)], axis=1
    )
    from_next = net.along(dkv_wide[:RIM], -1)
    from_prev = net.along(dkv_wide[rows + RIM :], 1)
    dkv = dkv_wide[RIM : RIM + rows]
    dkv = jnp.concatenate(
        [dkv[:RIM] + from_prev, dkv[RIM : rows - RIM], dkv[rows - RIM :] + from_next], axis=0
    )
    input_grad, sums_one = first_call(dq, dkv, states_low, d_mixed, mod, w_in)

    d_mod = jnp.concatenate([sums_one[:2], sums_two[:2]], axis=0).reshape(1, 4 * D)
    d_mod = net.sum_nodes(d_mod)[0]
    everyone = net.gather_noise(jnp.concatenate([d_mod, cond_low[0].astype(F32)]))
    conds = lax.dynamic_slice_in_dim(everyone[:, 4 * D :], device * own, own, 1)
    grad_mod = lax.dot_general(
        conds, everyone[:, : 4 * D], (((0,), (0,)), ((), ())), precision=lax.Precision.HIGHEST
    )

    results = [final[None], input_grad[None]]
    for weight, first, second, grads in (
        (inward_weight, inward_first, inward_second, net.reduce_rows(grad_in)),
        (outward_weight, outward_first, outward_second, net.reduce_rows(grad_out)),
        (expand_weight, expand_first, expand_second, net.reduce_rows(grad_exp)),
        (contract_weight, contract_first, contract_second, net.reduce_rows(grad_con)),
        (modulate_weight, modulate_first, modulate_second, grad_mod),
    ):
        results.extend(adamw(weight, first, second, grads))
    return tuple(results)


def solution(mesh):
    grid = P("noise", "nodes", None)
    shard = P("nodes", None)
    return jax.shard_map(
        per_device,
        mesh=mesh,
        in_specs=(grid, P("noise"), grid, grid) + (shard,) * 15,
        out_specs=(grid, grid) + (shard,) * 15,
        check_vma=False,
    )
```

time: 790 us -> 285 us (0.36)
  local copies, waits for them, and re-layouts: 255 us -> 30.3 us
  waiting for transfers between devices: 269 us -> 65.6 us
  matrix products: 161 us -> 21.9 us
  starting transfers between devices: 7.24 us -> 58 us
  Pallas kernels: 0 us -> 46.1 us
  other arithmetic: 56 us -> 28.3 us
    reduce_scatter x5 -> x0, waiting for transfers between devices: 163 us -> none  [the longest x1 51.4 us: per_device(): lax.psum_scatter(summed[3], 'nodes', scatter_dimension=0, tiled=True)]
    gather x4 -> x1, local copies, waits for them, and re-layouts: 142 us -> 0.83 us  [gather_noise(): return held[order]]
    dot_general x29 -> x9, matrix products: 161 us -> 21.9 us  [the longest x7 18.3 us: dot(): lax.dot_general(left, right, (((left_dim,), (right_dim,)), ((), ())), pre...]
    psum x1 -> x0, waiting for transfers between devices: 56.5 us -> none  [per_device(): lax.psum((grad_in, grad_out, grad_exp, grad_con, grad_mod), 'noise')]
    ppermute x4 -> x44, starting transfers between devices: 6.83 us -> 57.9 us  [the longest x40 50.6 us: permute(): return lax.ppermute(value, AXES, pairs)]
    pallas_call x0 -> x5, Pallas kernels: none -> 46.1 us  [the longest x1 19.8 us: mlp_call(): pl.pallas_call(mlp_kernel, grid=(rows // ROWS_MLP,), in_specs=[some(D), s...]
    ppermute x4 -> x44, waiting for transfers between devices: 0.32 us -> 26.3 us  [the longest x40 25.9 us: permute(): return lax.ppermute(value, AXES, pairs)]
    while x34 -> x0, local copies, waits for them, and re-layouts: 25.8 us -> none
  transfers between devices with their start and end apart: 14 -> 47, of which waited for: 8 -> 21; matrix products, arithmetic and copies ran while one was open for 54% -> 21% of each run, Pallas kernels for 0% -> 5%
where the time goes in v1:
time: 285 us; the launch traced here: 284 us
  waiting for transfers between devices  65.6 us (23%)
  starting transfers between devices  58 us (20%)
  Pallas kernels  46.1 us (16%)
  local copies, waits for them, and re-layouts  30.3 us (11%)
  other arithmetic  28.3 us (10%)
  matrix products  21.9 us (8%)
  blocking collectives  17.9 us (6%)
  between operations  15.6 us (5%)
    ppermute x40, starting transfers between devices, permute(): return lax.ppermute(value, AXES, pairs)  50.6 us
    all_gather x1, waiting for transfers between devices, per_device(): lax.all_gather(contract_weight.astype(BF16), 'nodes', axis=0, tiled=True)  30.8 us
    ppermute x40, waiting for transfers between devices, permute(): return lax.ppermute(value, AXES, pairs)  25.9 us
    pallas_call x1, Pallas kernels, mlp_call(): pl.pallas_call(mlp_kernel, grid=(rows // ROWS_MLP,), in_specs=[some(D), s...  19.8 us
    dot_general x7, matrix products, dot(): lax.dot_general(left, right, (((left_dim,), (right_dim,)), ((), ())), pre...  18.3 us
    all_gather x1, blocking collectives, per_device(): lax.all_gather(outward_weight.astype(BF16), 'nodes', axis=0, tiled=True)  17.9 us
    unnamed x115, local copies, waits for them, and re-layouts  14.4 us
    pallas_call x1, Pallas kernels, attend_back_call(): pl.pallas_call(attend_back_kernel, grid=(count + 1,), in_specs=[pl.BlockS...  11.3 us
  transfers between devices with their start and end apart: 47, of which 21 were waited for; matrix products, arithmetic and copies ran while one was open for 21% of the time, Pallas kernels for 5%

profile of v1, /device:TPU:0, one launch (start us, length us, event | category | flops | bytes accessed | tf_op | source)
XLA Modules:
  0.0 283.7 jit_solution(7122435090204827753)
XLA Ops:
  13.5 4.7 %collective-permute-start.1 = (bf16[64,512]{1,0:T(8,128)(2,1)S(1)}, bf16[64,512]{1,0:T(8,128)(2,1)S(1)}, u32[]{:S(2)}, u32[]{:S(2)}) collective-permute-start(bf16[64,512]{1,0:T(8,128)(2,1)S(1)} %get-tuple-element.75), channel_id=1, source_target_pairs={{0,7},{1,0},{2,1},{3,2},{4,3},{5,4},{6,5},{7,6},{8,15},{9,8},{10,9... | collective-permute-start | bytes 196616 | tf_op jit(solution)/shard_map/ppermute | solution.py:319
  18.4 17.9 %all_gather.13.w_out_ref = bf16[512,512]{1,0:T(8,128)(2,1)} all-gather(bf16[64,512]{1,0:T(8,128)(2,1)S(1)} %convert_element_type.288), channel_id=1, replica_groups=mesh['noise'=4,'nodes'=8] {'nodes'}, dimensions={0}, use_global_device_ids=true | all-gather | bytes 589824 | tf_op jit(solution)/shard_map/all_gather | solution.py:402
  37.3 3.0 %collective-permute-done.3 = f32[4,512]{1,0:T(4,128)S(1)} collective-permute-done((f32[4,512]{1,0:T(4,128)S(1)}, f32[4,512]{1,0:T(4,128)S(1)}, u32[]{:S(2)}, u32[]{:S(2)}) %collective-permute-start.3) | collective-permute-done | bytes 8224 | tf_op jit(solution)/shard_map/ppermute | solution.py:315
  41.8 3.2 %neighbour_counts.1.bias_ref = f32[1024,256]{1,0:T(8,128)S(1)} custom-call(s32[1024,16]{1,0:T(8,128)S(1)} %fusion.18.places_ref), custom_call_target="tpu_custom_call" | custom-call | flops 12582912 | bytes 1048576 | tf_op jit(solution)/shard_map/neighbour_counts/pallas_call | solution.py:79
  48.4 2.2 convolution_convert_fusion.4.q_ref
  50.7 3.0 %convolution_convert_fusion.low_ref.high_ref = bf16[1152,1024]{1,0:T(8,128)(2,1)S(1)} fusion(bf16[1152,512]{1,0:T(8,128)(2,1)} %fusion.5, bf16[512,1536]{1,0:T(8,128)(2,1)S(1)} %copy-done.10), kind=kOutput, calls=%fused_computation.1 | convolution fusion | flops 1209139200 | bytes 4587520 | tf_op jit(solution)/shard_map/dot_general | solution.py:26
  53.8 7.2 %attention_forward.1 = (bf16[1024,512]{1,0:T(8,128)(2,1)S(1)}, bf16[1024,1024]{1,0:T(8,128)(2,1)S(1)}) custom-call(bf16[1024,512]{1,0:T(8,128)(2,1)S(1)} %convolution_convert_fusion.4.q_ref, bf16[1152,1024]{1,0:T(8,128)(2,1)S(1)} %convolution_convert_fusion.low_ref.high_ref, bf16[1152,1024]{1,0:T(8,128)(2,1)S(1)} %convolution_convert_fusion.low_ref.high_ref, ...), custom_call_target="tpu_custom_call" | custom-call | flops 536870912 | bytes 6291456 | tf_op jit(solution)/shard_map/attention_forward/pallas_call | solution.py:109
  63.3 8.5 %all-gather.6.cloned.1.call-done.w_exp_ref = bf16[512,2048]{1,0:T(8,128)(2,1)} async-done(((bf16[64,2048]{1,0:T(8,128)(2,1)}), bf16[512,2048]{1,0:T(8,128)(2,1)}) %all-gather.6.cloned.1.call-update) | async-done | bytes 2097168 | tf_op jit(solution)/shard_map/all_gather | solution.py:403
  71.8 30.8 %all-gather.8.cloned.1.call-done.w_con_ref = bf16[2048,512]{1,0:T(8,128)(2,1)} async-done(((bf16[256,512]{1,0:T(8,128)(2,1)}), bf16[2048,512]{1,0:T(8,128)(2,1)}) %all-gather.8.cloned.1.call-update) | async-done | bytes 2097168 | tf_op jit(solution)/shard_map/all_gather | solution.py:404
  106.1 19.8 %mlp.1 = (bf16[1024,512]{1,0:T(8,128)(2,1)}, bf16[1024,512]{1,0:T(8,128)(2,1)S(1)}, bf16[1024,2048]{1,0:T(8,128)(2,1)}, bf16[1024,2048]{1,0:T(8,128)(2,1)}, f32[...) custom-call(bf16[1024,512]{1,0:T(8,128)(2,1)S(1)} %copy-done.15, ...), custom_call_target="tpu_custom_call" | custom-call | flops 9663676416 | bytes 23068672 | tf_op jit(solution)/shard_map/mlp/pallas_call | solution.py:247
  126.0 11.3 %attention_backward.1 = (bf16[1024,512]{1,0:T(8,128)(2,1)S(1)}, bf16[1152,1024]{1,0:T(8,128)(2,1)S(1)}) custom-call(bf16[1024,512]{1,0:T(8,128)(2,1)S(1)} %copy-done.5, bf16[1152,1024]{1,0:T(8,128)(2,1)S(1)} %convolution_convert_fusion.low_ref.high_ref, bf16[1152,1024]{1,0:T(8,128)(2,1)S(1)} %convolution_convert_fusion.low_ref.high_ref, ...), custom_call_target="tpu_custom_call" | custom-call | flops 1073741824 | bytes 10485760 | tf_op jit(solution)/shard_map/attention_backward/pallas_call | solution.py:174
  138.1 3.3 %convolution_convert_fusion.3 = bf16[512,1024]{1,0:T(8,128)(2,1)S(1)} fusion(bf16[1152,512]{1,0:T(8,128)(2,1)} %fusion.5, bf16[1152,1024]{1,0:T(8,128)(2,1)S(1)} %get-tuple-element.35), kind=kOutput, calls=%fused_computation.23 | convolution fusion | flops 1208483840 | bytes 4587520 | tf_op jit(solution)/shard_map/dot_general | solution.py:26
  141.9 2.4 convolution_convert_fusion.1
  145.8 2.4 copy.44
  149.5 4.6 %convolution_convert_fusion.2 = bf16[512,2048]{1,0:T(8,128)(2,1)S(1)} fusion(bf16[1024,512]{1,0:T(8,128)(2,1)S(1)} %copy-done.21, bf16[1024,2048]{1,0:T(8,128)(2,1)} %get-tuple-element.39), kind=kOutput, calls=%fused_computation.3 | convolution fusion | flops 2148532224 | bytes 7340032 | tf_op jit(solution)/shard_map/dot_general | solution.py:26
  159.5 2.0 collective-permute-start.6
  161.5 1.9 convolution_convert_fusion.6
  165.5 4.5 %input_gradient.1 = (f32[1024,512]{1,0:T(8,128)}, f32[8,512]{1,0:T(8,128)S(1)}) custom-call(bf16[1024,512]{1,0:T(8,128)(2,1)S(1)} %copy-done.13, bf16[1024,1024]{1,0:T(8,128)(2,1)S(1)} %pad_maximum_fusion.dkv_ref, bf16[1024,512]{1,0:T(8,128)(2,1)S(1)} %bitcast.254, f32[1024,512]{1,0:T(8,128)S(1)} %copy-done.3, f32[4,512]{1,0:T(4,128)S(1)} %add.394.mod_ref, ...), custom_call_target="tpu_custom_call" | custom-call | flops 1610612736 | bytes 10485760 | tf_op jit(solution)/shard_map/input_gradient/pallas_call | solution.py:288
  175.0 2.3 collective-permute-start.41
  186.4 2.9 %collective-permute-start.19 = (bf16[64,128]{1,0:T(8,128)(2,1)S(1)}, bf16[64,128]{1,0:T(8,128)(2,1)S(1)}, u32[]{:S(2)}, u32[]{:S(2)}) collective-permute-start(bf16[64,128]{1,0:T(8,128)(2,1)S(1)} %get-tuple-element.115), channel_id=1, source_target_pairs={{0,4},{1,5},{2,6},{3,7},{4,0},{5,1},{6,2},{7,3},{8,12},{9,13},{10,... | collective-permute-start | bytes 49160 | tf_op jit(solution)/shard_map/ppermute | solution.py:315
  199.0 3.4 %multiply_subtract_fusion = (f32[64,2048]{1,0:T(8,128)}, f32[64,2048]{1,0:T(8,128)}, f32[64,2048]{1,0:T(8,128)}) fusion(f32[64,2048]{1,0:T(8,128)S(1)} %copy-done.33, f32[64,2048]{1,0:T(8,128)} %param.36, f32[64,2048]{1,0:T(8,128)} %param.37, f32[4,2560]{1,0:T(4,128)} %copy-done.48, f32[4,512]{1,0:T(4,128)S(1)} %slice.232, s32[]{:T(128)S(6)} %select_n.227), kind=kOutput, calls=%fused_computation.73 | convolution fusion | flops 8126464 | bytes 3180548 | tf_op jit(solution)/shard_map/dot_general | solution.py:448
  203.3 2.3 fusion.8
  221.2 1.9 fusion.7
  227.7 2.4 collective-permute-start.11
  230.1 2.1 collective-permute-start.12
  232.2 2.4 constant_dynamic-slice_fusion.11
  236.9 2.7 collective-permute-done.13
  242.4 6.5 %collective-permute-done.24 = bf16[2,4,64,512]{3,2,1,0:T(8,128)(2,1)S(1)} collective-permute-done((bf16[2,4,64,512]{3,2,1,0:T(8,128)(2,1)S(1)}, bf16[2,4,64,512]{3,2,1,0:T(8,128)(2,1)S(1)}, u32[]{:S(2)}, u32[]{:S(2)}) %collective-permute-start.24) | collective-permute-done | bytes 524320 | tf_op jit(solution)/shard_map/ppermute | solution.py:315
  249.1 2.1 collective-permute-start.25
  259.2 1.9 collective-permute-start.28
  268.7 1.9 collective-permute-start.30
  270.9 2.9 %collective-permute-done.30 = bf16[2,64,512]{2,1,0:T(8,128)(2,1)S(1)} collective-permute-done((bf16[2,64,512]{2,1,0:T(8,128)(2,1)S(1)}, bf16[2,64,512]{2,1,0:T(8,128)(2,1)S(1)}, u32[]{:S(2)}, u32[]{:S(2)}) %collective-permute-start.30) | collective-permute-done | bytes 131104 | tf_op jit(solution)/shard_map/ppermute | solution.py:315
  (300 shorter events, 97.4 us)
Async XLA Ops:
  7.2 41.2 %all-gather.4.cloned.1.call-start = ((), (), s32[]{:S(2)}) async-start(), calls=%async_computation | async-start | bytes 1769472 | tf_op jit(solution)/shard_map/all_gather | solution.py:401
  9.1 62.7 %all-gather.6.cloned.1.call-start = ((), (), s32[]{:S(2)}) async-start(), calls=%async_computation.1 | async-start | bytes 2359296 | tf_op jit(solution)/shard_map/all_gather | solution.py:403
  11.0 91.7 %all-gather.8.cloned.1.call-start = ((), (), s32[]{:S(2)}) async-start(), calls=%async_computation.2 | async-start | bytes 2359296 | tf_op jit(solution)/shard_map/all_gather | solution.py:404
  12.8 23.7 %collective-permute-start.2 = (f32[4,512]{1,0:T(4,128)S(1)}, f32[4,512]{1,0:T(4,128)S(1)}, u32[]{:S(2)}, u32[]{:S(2)}) collective-permute-start(f32[4,512]{1,0:T(4,128)S(1)} %bitcast.305), channel_id=1, source_target_pairs={{0,1},{1,0},{2,3},{3,2},{4,5},{5,4},{6,7},{7,6},{8,9},{9,8},{10,11... | collective-permute-start | bytes 24584 | tf_op jit(solution)/shard_map/ppermute | solution.py:315
  13.4 32.7 %collective-permute-start = (bf16[64,512]{1,0:T(8,128)(2,1)S(1)}, bf16[64,512]{1,0:T(8,128)(2,1)S(1)}, u32[]{:S(2)}, u32[]{:S(2)}) collective-permute-start(bf16[64,512]{1,0:T(8,128)(2,1)S(1)} %get-tuple-element.74), channel_id=1, source_target_pairs={{0,1},{1,2},{2,3},{3,4},{4,5},{5,6},{6,7},{7,0},{8,9},{9,10},{10,1... | collective-permute-start | bytes 196616 | tf_op jit(solution)/shard_map/ppermute | solution.py:319
  13.5 32.6 %collective-permute-start.1 = (bf16[64,512]{1,0:T(8,128)(2,1)S(1)}, bf16[64,512]{1,0:T(8,128)(2,1)S(1)}, u32[]{:S(2)}, u32[]{:S(2)}) collective-permute-start(bf16[64,512]{1,0:T(8,128)(2,1)S(1)} %get-tuple-element.75), channel_id=1, source_target_pairs={{0,7},{1,0},{2,1},{3,2},{4,3},{5,4},{6,5},{7,6},{8,15},{9,8},{10,9... | collective-permute-start | bytes 196616 | tf_op jit(solution)/shard_map/ppermute | solution.py:319
  40.3 5.7 %collective-permute-start.4 = (f32[4,512]{1,0:T(4,128)S(1)}, f32[4,512]{1,0:T(4,128)S(1)}, u32[]{:S(2)}, u32[]{:S(2)}) collective-permute-start(f32[4,512]{1,0:T(4,128)S(1)} %add.393), channel_id=1, source_target_pairs={{0,4},{1,5},{2,6},{3,7},{4,0},{5,1},{6,2},{7,3},{8,12},{9,13},{10,... | collective-permute-start | bytes 24584 | tf_op jit(solution)/shard_map/ppermute | solution.py:315
  141.4 16.3 %collective-permute-start.5 = (bf16[64,1024]{1,0:T(8,128)(2,1)}, bf16[64,1024]{1,0:T(8,128)(2,1)}, u32[]{:S(2)}, u32[]{:S(2)}) collective-permute-start(bf16[64,1024]{1,0:T(8,128)(2,1)} %slice.169), channel_id=1, source_target_pairs={{0,1},{1,2},{2,3},{3,4},{4,5},{5,6},{6,7},{7,0},{8,9},{9,10},{10,1... | collective-permute-start | bytes 393224 | tf_op jit(solution)/shard_map/ppermute | solution.py:319
  148.1 63.2 %collective-permute-start.31 = (bf16[4,256,512]{1,2,0:T(8,128)(2,1)}, bf16[4,256,512]{1,2,0:T(8,128)(2,1)}, u32[]{:S(2)}, u32[]{:S(2)}) collective-permute-start(bf16[4,256,512]{1,2,0:T(8,128)(2,1)} %bitcast.267), channel_id=1, source_target_pairs={{0,1},{1,0},{2,3},{3,2},{4,5},{5,4},{6,7},{7,6},{8,9},{9,8},{10,11... | collective-permute-start | bytes 3145736 | tf_op jit(solution)/shard_map/ppermute | solution.py:315
  155.2 65.9 %collective-permute-start.23 = (bf16[4,64,2048]{2,1,0:T(8,128)(2,1)}, bf16[4,64,2048]{2,1,0:T(8,128)(2,1)}, u32[]{:S(2)}, u32[]{:S(2)}) collective-permute-start(bf16[4,64,2048]{2,1,0:T(8,128)(2,1)} %dynamic-slice_bitcast_fusion), channel_id=1, source_target_pairs={{0,1},{1,0},{2,3},{3,2},{4,5},{5,4},{6,7},{7,6},{8,9},{9,8},{10,11... | collective-permute-start | bytes 3145736 | tf_op jit(solution)/shard_map/ppermute | solution.py:315
  157.7 12.4 %collective-permute-start.15 = (bf16[4,64,512]{2,1,0:T(8,128)(2,1)S(1)}, bf16[4,64,512]{2,1,0:T(8,128)(2,1)S(1)}, u32[]{:S(2)}, u32[]{:S(2)}) collective-permute-start(bf16[4,64,512]{2,1,0:T(8,128)(2,1)S(1)} %dynamic-slice_bitcast_fusion.1), channel_id=1, source_target_pairs={{0,1},{1,0},{2,3},{3,2},{4,5},{5,4},{6,7},{7,6},{8,9},{9,8},{10,11... | collective-permute-start | bytes 786440 | tf_op jit(solution)/shard_map/ppermute | solution.py:315
  171.9 7.7 %collective-permute-start.16 = (bf16[2,4,64,128]{3,2,1,0:T(8,128)(2,1)S(1)}, bf16[2,4,64,128]{3,2,1,0:T(8,128)(2,1)}, u32[]{:S(2)}, u32[]{:S(2)}) collective-permute-start(bf16[2,4,64,128]{3,2,1,0:T(8,128)(2,1)S(1)} %pad_maximum_fusion.11), channel_id=1, source_target_pairs={{0,8},{1,17},{2,10},{3,19},{4,12},{5,21},{6,14},{7,23},{8,0},{9,25... | collective-permute-start | bytes 393224 | tf_op jit(solution)/shard_map/ppermute | solution.py:315
  182.8 6.5 %collective-permute-start.42 = (f32[1,2560]{1,0:T(1,128)S(1)}, f32[1,2560]{1,0:T(1,128)S(1)}, u32[]{:S(2)}, u32[]{:S(2)}) collective-permute-start(f32[1,2560]{1,0:T(1,128)S(1)} %broadcast_in_dim.8), channel_id=1, source_target_pairs={{0,8},{1,9},{2,10},{3,11},{4,12},{5,13},{6,14},{7,15},{8,0},{9,1},... | collective-permute-start | bytes 30728 | tf_op jit(solution)/shard_map/ppermute | solution.py:315
  185.0 5.6 %collective-permute-start.18 = (bf16[64,128]{1,0:T(8,128)(2,1)S(1)}, bf16[64,128]{1,0:T(8,128)(2,1)S(1)}, u32[]{:S(2)}, u32[]{:S(2)}) collective-permute-start(bf16[64,128]{1,0:T(8,128)(2,1)S(1)} %get-tuple-element.113), channel_id=1, source_target_pairs={{0,2},{1,3},{2,4},{3,5},{4,6},{5,7},{6,0},{7,1},{8,10},{9,11},{10,... | collective-permute-start | bytes 49160 | tf_op jit(solution)/shard_map/ppermute | solution.py:315
  190.6 12.8 %collective-permute-start.7 = (bf16[4,64,1536]{2,1,0:T(8,128)(2,1)}, bf16[4,64,1536]{2,1,0:T(8,128)(2,1)}, u32[]{:S(2)}, u32[]{:S(2)}) collective-permute-start(bf16[4,64,1536]{2,1,0:T(8,128)(2,1)} %fusion.14), channel_id=1, source_target_pairs={{0,1},{1,0},{2,3},{3,2},{4,5},{5,4},{6,7},{7,6},{8,9},{9,8},{10,11... | collective-permute-start | bytes 2359304 | tf_op jit(solution)/shard_map/ppermute | solution.py:315
  197.5 4.9 %collective-permute-start.22 = (bf16[2,64,128]{2,1,0:T(8,128)(2,1)S(1)}, bf16[2,64,128]{2,1,0:T(8,128)(2,1)S(1)}, u32[]{:S(2)}, u32[]{:S(2)}) collective-permute-start(bf16[2,64,128]{2,1,0:T(8,128)(2,1)S(1)} %pad_maximum_fusion.18), channel_id=1, source_target_pairs={{0,8},{1,17},{2,10},{3,19},{4,12},{5,21},{6,14},{7,23},{8,0},{9,25... | collective-permute-start | bytes 98312 | tf_op jit(solution)/shard_map/ppermute | solution.py:315
  209.3 7.8 %collective-permute-start.8 = (bf16[2,4,64,384]{3,2,1,0:T(8,128)(2,1)S(1)}, bf16[2,4,64,384]{3,2,1,0:T(8,128)(2,1)S(1)}, u32[]{:S(2)}, u32[]{:S(2)}) collective-permute-start(bf16[2,4,64,384]{3,2,1,0:T(8,128)(2,1)S(1)} %pad_maximum_fusion.4), channel_id=1, source_target_pairs={{0,8},{1,17},{2,10},{3,19},{4,12},{5,21},{6,14},{7,23},{8,0},{9,25... | collective-permute-start | bytes 1179656 | tf_op jit(solution)/shard_map/ppermute | solution.py:315
  214.2 26.0 %collective-permute-start.32 = (bf16[2,4,256,128]{3,2,1,0:T(8,128)(2,1)}, bf16[2,4,256,128]{3,2,1,0:T(8,128)(2,1)}, u32[]{:S(2)}, u32[]{:S(2)}) collective-permute-start(bf16[2,4,256,128]{3,2,1,0:T(8,128)(2,1)} %pad_maximum_fusion.3), channel_id=1, source_target_pairs={{0,8},{1,17},{2,10},{3,19},{4,12},{5,21},{6,14},{7,23},{8,0},{9,25... | collective-permute-start | bytes 1572872 | tf_op jit(solution)/shard_map/ppermute | solution.py:315
  219.7 6.0 %collective-permute-start.9 = (bf16[4,64,384]{2,1,0:T(8,128)(2,1)}, bf16[4,64,384]{2,1,0:T(8,128)(2,1)}, u32[]{:S(2)}, u32[]{:S(2)}) collective-permute-start(bf16[4,64,384]{2,1,0:T(8,128)(2,1)} %fusion.39), channel_id=1, source_target_pairs={{0,16},{1,9},{2,18},{3,11},{4,20},{5,13},{6,22},{7,15},{8,24},{9,1... | collective-permute-start | bytes 589832 | tf_op jit(solution)/shard_map/ppermute | solution.py:315
  226.8 8.0 %collective-permute-start.10 = (bf16[64,384]{1,0:T(8,128)(2,1)S(1)}, bf16[64,384]{1,0:T(8,128)(2,1)S(1)}, u32[]{:S(2)}, u32[]{:S(2)}) collective-permute-start(bf16[64,384]{1,0:T(8,128)(2,1)S(1)} %get-tuple-element.106), channel_id=1, source_target_pairs={{0,2},{1,3},{2,4},{3,5},{4,6},{5,7},{6,0},{7,1},{8,10},{9,11},{10,... | collective-permute-start | bytes 147464 | tf_op jit(solution)/shard_map/ppermute | solution.py:315
  227.7 7.0 %collective-permute-start.11 = (bf16[64,384]{1,0:T(8,128)(2,1)S(1)}, bf16[64,384]{1,0:T(8,128)(2,1)S(1)}, u32[]{:S(2)}, u32[]{:S(2)}) collective-permute-start(bf16[64,384]{1,0:T(8,128)(2,1)S(1)} %get-tuple-element.108), channel_id=1, source_target_pairs={{0,4},{1,5},{2,6},{3,7},{4,0},{5,1},{6,2},{7,3},{8,12},{9,13},{10,... | collective-permute-start | bytes 147464 | tf_op jit(solution)/shard_map/ppermute | solution.py:315
  236.3 12.6 %collective-permute-start.24 = (bf16[2,4,64,512]{3,2,1,0:T(8,128)(2,1)S(1)}, bf16[2,4,64,512]{3,2,1,0:T(8,128)(2,1)S(1)}, u32[]{:S(2)}, u32[]{:S(2)}) collective-permute-start(bf16[2,4,64,512]{3,2,1,0:T(8,128)(2,1)S(1)} %pad_maximum_fusion.2), channel_id=1, source_target_pairs={{0,8},{1,17},{2,10},{3,19},{4,12},{5,21},{6,14},{7,23},{8,0},{9,25... | collective-permute-start | bytes 1572872 | tf_op jit(solution)/shard_map/ppermute | solution.py:315
  239.6 11.5 %collective-permute-start.14 = (bf16[2,64,384]{2,1,0:T(8,128)(2,1)S(1)}, bf16[2,64,384]{2,1,0:T(8,128)(2,1)S(1)}, u32[]{:S(2)}, u32[]{:S(2)}) collective-permute-start(bf16[2,64,384]{2,1,0:T(8,128)(2,1)S(1)} %pad_maximum_fusion.14), channel_id=1, source_target_pairs={{0,8},{1,17},{2,10},{3,19},{4,12},{5,21},{6,14},{7,23},{8,0},{9,25... | collective-permute-start | bytes 294920 | tf_op jit(solution)/shard_map/ppermute | solution.py:315
  241.4 9.9 %collective-permute-start.33 = (bf16[4,256,128]{2,1,0:T(8,128)(2,1)S(1)}, bf16[4,256,128]{2,1,0:T(8,128)(2,1)S(1)}, u32[]{:S(2)}, u32[]{:S(2)}) collective-permute-start(bf16[4,256,128]{2,1,0:T(8,128)(2,1)S(1)} %fusion.35), channel_id=1, source_target_pairs={{0,16},{1,9},{2,18},{3,11},{4,20},{5,13},{6,22},{7,15},{8,24},{9,1... | collective-permute-start | bytes 786440 | tf_op jit(solution)/shard_map/ppermute | solution.py:315
  249.1 6.9 %collective-permute-start.25 = (bf16[4,64,512]{2,1,0:T(8,128)(2,1)S(1)}, bf16[4,64,512]{2,1,0:T(8,128)(2,1)S(1)}, u32[]{:S(2)}, u32[]{:S(2)}) collective-permute-start(bf16[4,64,512]{2,1,0:T(8,128)(2,1)S(1)} %fusion.34), channel_id=1, source_target_pairs={{0,16},{1,9},{2,18},{3,11},{4,20},{5,13},{6,22},{7,15},{8,24},{9,1... | collective-permute-start | bytes 786440 | tf_op jit(solution)/shard_map/ppermute | solution.py:315
  251.5 7.8 %collective-permute-start.34 = (bf16[256,128]{1,0:T(8,128)(2,1)S(1)}, bf16[256,128]{1,0:T(8,128)(2,1)S(1)}, u32[]{:S(2)}, u32[]{:S(2)}) collective-permute-start(bf16[256,128]{1,0:T(8,128)(2,1)S(1)} %get-tuple-element.87), channel_id=1, source_target_pairs={{0,2},{1,3},{2,4},{3,5},{4,6},{5,7},{6,0},{7,1},{8,10},{9,11},{10,... | collective-permute-start | bytes 196616 | tf_op jit(solution)/shard_map/ppermute | solution.py:315
  252.7 8.4 %collective-permute-start.35 = (bf16[256,128]{1,0:T(8,128)(2,1)S(1)}, bf16[256,128]{1,0:T(8,128)(2,1)S(1)}, u32[]{:S(2)}, u32[]{:S(2)}) collective-permute-start(bf16[256,128]{1,0:T(8,128)(2,1)S(1)} %get-tuple-element.89), channel_id=1, source_target_pairs={{0,4},{1,5},{2,6},{3,7},{4,0},{5,1},{6,2},{7,3},{8,12},{9,13},{10,... | collective-permute-start | bytes 196616 | tf_op jit(solution)/shard_map/ppermute | solution.py:315
  254.4 6.7 %collective-permute-start.36 = (bf16[256,128]{1,0:T(8,128)(2,1)S(1)}, bf16[256,128]{1,0:T(8,128)(2,1)S(1)}, u32[]{:S(2)}, u32[]{:S(2)}) collective-permute-start(bf16[256,128]{1,0:T(8,128)(2,1)S(1)} %get-tuple-element.88), channel_id=1, source_target_pairs={{0,6},{1,7},{2,0},{3,1},{4,2},{5,3},{6,4},{7,5},{8,14},{9,15},{10,... | collective-permute-start | bytes 196616 | tf_op jit(solution)/shard_map/ppermute | solution.py:315
  256.3 6.2 %collective-permute-start.26 = (bf16[64,512]{1,0:T(8,128)(2,1)S(1)}, bf16[64,512]{1,0:T(8,128)(2,1)S(1)}, u32[]{:S(2)}, u32[]{:S(2)}) collective-permute-start(bf16[64,512]{1,0:T(8,128)(2,1)S(1)} %get-tuple-element.94), channel_id=1, source_target_pairs={{0,2},{1,3},{2,4},{3,5},{4,6},{5,7},{6,0},{7,1},{8,10},{9,11},{10,... | collective-permute-start | bytes 196616 | tf_op jit(solution)/shard_map/ppermute | solution.py:315
  257.8 6.1 %collective-permute-start.27 = (bf16[64,512]{1,0:T(8,128)(2,1)S(1)}, bf16[64,512]{1,0:T(8,128)(2,1)S(1)}, u32[]{:S(2)}, u32[]{:S(2)}) collective-permute-start(bf16[64,512]{1,0:T(8,128)(2,1)S(1)} %get-tuple-element.96), channel_id=1, source_target_pairs={{0,4},{1,5},{2,6},{3,7},{4,0},{5,1},{6,2},{7,3},{8,12},{9,13},{10,... | collective-permute-start | bytes 196616 | tf_op jit(solution)/shard_map/ppermute | solution.py:315
  265.7 5.0 %collective-permute-start.38 = (bf16[2,256,128]{2,1,0:T(8,128)(2,1)S(1)}, bf16[2,256,128]{2,1,0:T(8,128)(2,1)S(1)}, u32[]{:S(2)}, u32[]{:S(2)}) collective-permute-start(bf16[2,256,128]{2,1,0:T(8,128)(2,1)S(1)} %pad_maximum_fusion.13), channel_id=1, source_target_pairs={{0,8},{1,17},{2,10},{3,19},{4,12},{5,21},{6,14},{7,23},{8,0},{9,25... | collective-permute-start | bytes 393224 | tf_op jit(solution)/shard_map/ppermute | solution.py:315
  268.7 5.0 %collective-permute-start.30 = (bf16[2,64,512]{2,1,0:T(8,128)(2,1)S(1)}, bf16[2,64,512]{2,1,0:T(8,128)(2,1)S(1)}, u32[]{:S(2)}, u32[]{:S(2)}) collective-permute-start(bf16[2,64,512]{2,1,0:T(8,128)(2,1)S(1)} %pad_maximum_fusion.12), channel_id=1, source_target_pairs={{0,8},{1,17},{2,10},{3,19},{4,12},{5,21},{6,14},{7,23},{8,0},{9,25... | collective-permute-start | bytes 393224 | tf_op jit(solution)/shard_map/ppermute | solution.py:315
  (65 other events, 375.5 us)
Sparse Core Ops, SparseCore 0:
  10.3 30.4 all-gather.3
  43.0 28.7 all-gather.5
  74.0 28.5 all-gather.7
